TPU v7x, 32 devices: a whole 2x2x4 slice. The times are simulated.
32 devices in a mesh: chain: 4 (over z), cross: 4 (over y, x), real: 2 (over core).
Axes of the slice: x: 2, y: 2, z: 4, core: 2. Of those that a mesh axis runs over, the one named last changes fastest.
Arguments:
- velocity_u: float32 [32, 256, 512], P('real', 'chain', 'cross'), may hold values from -4 to 4
- velocity_w: float32 [32, 256, 512], P('real', 'chain', 'cross'), may hold values from -4 to 4
- stress_uu: float32 [32, 256, 512], P('real', 'chain', 'cross'), may hold values from -6 to 6
- stress_ww: float32 [32, 256, 512], P('real', 'chain', 'cross'), may hold values from -6 to 6
- stress_uw: float32 [32, 256, 512], P('real', 'chain', 'cross'), may hold values from -6 to 6
- basis: float32 [48, 256, 512], P('real', 'chain', 'cross'), may hold values from -0.875 to 0.875
- coefficients: float32 [2, 32, 48], replicated, may hold values from -5 to 5
Outputs:
- velocity_u_out: float32 [32, 256, 512], P('real', 'chain', 'cross')
- velocity_w_out: float32 [32, 256, 512], P('real', 'chain', 'cross')
- stress_uu_out: float32 [32, 256, 512], P('real', 'chain', 'cross')
- stress_ww_out: float32 [32, 256, 512], P('real', 'chain', 'cross')
- stress_uw_out: float32 [32, 256, 512], P('real', 'chain', 'cross')
All inputs are finite; a program needn't handle non-finite values.
Results may differ from a plain program's by a relative error of at most 0.00022.
Values sent between devices are 32-bit elements; how exact they have to be, the bound alone decides.
A program may use at most 128 MiB of HBM per device.

v0:
```python
import functools
import math

import jax
import jax.numpy as jnp
from jax import lax
from jax.experimental import pallas as pl
from jax.experimental.pallas import tpu as pltpu
from jax.sharding import PartitionSpec as P

STEPS = 6
time_step = 0.8
damping = 0.8
gravity = 0.1
modulus_m = 1.8
modulus_l = 0.6
modulus_g = 0.6

MESH = pl.DeviceIdType.MESH
LANES = 128
PART = 8
TOP = 8
PIECES = 4

SINE = [(math.sin(0.6), math.cos(0.6), -math.sin(0.6), -math.cos(0.6))[n % 4] * 0.25**n / math.factorial(n) for n in range(8)]
COSINE = [(math.cos(0.6), -math.sin(0.6), -math.cos(0.6), math.sin(0.6))[n % 4] * 0.25**n / math.factorial(n) for n in range(8)]


def horner(coefs, t):
    total = jnp.full_like(t, coefs[-1])
    for c in coefs[-2::-1]:
        total = total * t + c
    return total


def kernel(
    sizes, vu_in, vw_in, suu_in, sww_in, suw_in, basis_in, coef_in,
    vu_out, vw_out, suu_out, sww_out, suw_out,
    vu, vw, suu, sww, suw, strength, sine, basis, panel,
    xsend, xrecv, ysend, yrecv,
    xs_sem, xr_sem, ys_sem, yr_sem, bs_sem, br_sem, own_sem,
):
    n_chain, n_cross, n_real, cells_x, cells_y, realiz, modes = sizes
    slabs = cells_x // PART
    last = slabs
    rows = cells_y // PIECES
    ci, xi, ri = lax.axis_index("chain"), lax.axis_index("cross"), lax.axis_index("real")
    has = {
        ("chain", 0): ci > 0, ("chain", 1): ci < n_chain - 1,
        ("cross", 0): xi > 0, ("cross", 1): xi < n_cross - 1,
    }
    beside = {
        ("chain", 0): ci - 1, ("chain", 1): ci + 1,
        ("cross", 0): xi - 1, ("cross", 1): xi + 1,
    }

    xrecv[...] = jnp.zeros_like(xrecv)
    yrecv[...] = jnp.zeros_like(yrecv)

    barrier = pltpu.get_barrier_semaphore()
    for key in has:
        @pl.when(has[key])
        def _(key=key):
            pl.semaphore_signal(barrier, inc=1, device_id={key[0]: beside[key]}, device_id_type=MESH)
    for d in range(1, n_real):
        pl.semaphore_signal(barrier, inc=1, device_id={"real": lax.rem(ri + d, n_real)}, device_id_type=MESH)
    greeted = n_real - 1
    for key in has:
        greeted = greeted + has[key].astype(jnp.int32)
    pl.semaphore_wait(barrier, greeted)

    block = basis_in.shape[0]
    place = pl.ds(pl.multiple_of(ri * block, 8), block)
    sends = []
    for d in range(1, n_real):
        copy = pltpu.make_async_remote_copy(
            basis_in, basis.at[place], bs_sem.at[d - 1], br_sem.at[d - 1],
            device_id={"real": lax.rem(ri + d, n_real)}, device_id_type=MESH)
        copy.start()
        sends.append(copy)
    own = pltpu.make_async_copy(basis_in, basis.at[place], own_sem)
    own.start()

    slot_of = lax.broadcasted_iota(jnp.int32, (rows, LANES), 1) % PART

    def x_copy(side, slot):
        return pltpu.make_async_remote_copy(
            xsend.at[side, slot], xrecv.at[1 - side, slot], xs_sem.at[side, slot], xr_sem.at[1 - side, slot],
            device_id={"chain": beside[("chain", side)]}, device_id_type=MESH)

    def y_copy(side, slot):
        return pltpu.make_async_remote_copy(
            ysend.at[side, slot], yrecv.at[1 - side, slot], ys_sem.at[side, slot], yr_sem.at[1 - side, slot],
            device_id={"cross": beside[("cross", side)]}, device_id_type=MESH)

    def send_x(slot, fields):
        for side in range(2):
            slab = (1, last)[side]
            packed = jnp.zeros((rows, LANES), jnp.float32)
            for j in range(2 * PIECES):
                part = fields[j // PIECES][slab, pl.ds(TOP + (j % PIECES) * rows, rows), :]
                shift = (j - (0, PART - 1)[side]) % LANES
                packed = jnp.where(slot_of == j, pltpu.roll(part, shift, 1) if shift else part, packed)
            xsend[side, slot] = packed

            @pl.when(has[("chain", side)])
            def _(side=side):
                x_copy(side, slot).start()

    def send_y(slot, fields):
        for side in range(2):
            row = (TOP, TOP + cells_y - 1)[side]
            for f in range(2):
                for i in range(slabs):
                    ysend[side, slot, pl.ds(f * slabs + i, 1), :] = fields[f][1 + i, pl.ds(row, 1), :]

            @pl.when(has[("cross", side)])
            def _(side=side):
                y_copy(side, slot).start()

    def receive_x(slot, fields):
        for side in range(2):
            @pl.when(has[("chain", side)])
            def _(side=side):
                x_copy(side, slot).wait_send()
                pltpu.make_async_remote_copy(
                    xsend.at[1 - side, slot], xrecv.at[side, slot], xs_sem.at[1 - side, slot], xr_sem.at[side, slot],
                    device_id={"chain": beside[("chain", side)]}, device_id_type=MESH).wait_recv()
        for side in range(2):
            got = xrecv[side, slot]
            slab, ghost = ((last, 0), (1, last + 1))[side]
            edge = (0, PART - 1)[side]
            for j in range(2 * PIECES):
                at = pl.ds(TOP + (j % PIECES) * rows, rows)
                mine = pltpu.roll(fields[j // PIECES][slab, at, :], (1, LANES - 1)[side], 1)
                shift = (edge - j) % LANES
                theirs = pltpu.roll(got, shift, 1) if shift else got
                fields[j // PIECES][ghost, at, :] = jnp.where(slot_of == edge, theirs, mine)

    def receive_y(slot, fields):
        for side in range(2):
            @pl.when(has[("cross", side)])
            def _(side=side):
                y_copy(side, slot).wait_send()
                pltpu.make_async_remote_copy(
                    ysend.at[1 - side, slot], yrecv.at[side, slot], ys_sem.at[1 - side, slot], yr_sem.at[side, slot],
                    device_id={"cross": beside[("cross", side)]}, device_id_type=MESH).wait_recv()
        for side in range(2):
            row = (TOP - 1, TOP + cells_y)[side]
            for f in range(2):
                for i in range(slabs):
                    fields[f][1 + i, pl.ds(row, 1), :] = yrecv[side, slot, pl.ds(f * slabs + i, 1), :]

    whole = pl.ds(TOP, cells_y)
    for source, field in ((suu_in, suu), (sww_in, sww), (suw_in, suw)):
        def turn(i, _, source=source, field=field):
            field[1 + i, whole, :] = source[pl.ds(i, LANES, stride=PART), :].T
            return 0
        lax.fori_loop(0, slabs, turn, 0)
    send_x(0, (suu, suw))
    send_y(0, (suw, sww))
    for source, field in ((vu_in, vu), (vw_in, vw)):
        def turn(i, _, source=source, field=field):
            field[1 + i, whole, :] = source[pl.ds(i, LANES, stride=PART), :].T
            return 0
        lax.fori_loop(0, slabs, turn, 0)

    own.wait()
    for copy in sends:
        copy.wait()
    weights = jnp.concatenate([coef_in[f, pl.ds(pl.multiple_of(ri * realiz, 8), realiz), :] for f in range(2)], axis=0)
    weights_high = weights.astype(jnp.bfloat16)
    weights_low = (weights - weights_high.astype(jnp.float32)).astype(jnp.bfloat16)
    both = jnp.concatenate([weights_high, weights_low], axis=0)
    half = 2 * realiz

    def material(i, _):
        for part in range(PART):
            values = basis[pl.ds(part * PART + i, modes, stride=cells_x), :]
            high = values.astype(jnp.bfloat16)
            low = (values - high.astype(jnp.float32)).astype(jnp.bfloat16)
            product = jnp.dot(both, jnp.concatenate([high, low], axis=1), preferred_element_type=jnp.float32)
            sums = product[:half, :cells_y] + (product[:half, cells_y:] + product[half:, :cells_y])
            panel[pl.ds(part, half, stride=PART), :] = sums
        field_c = panel[pl.ds(0, LANES), :].T
        field_f = panel[pl.ds(LANES, LANES), :].T
        t = jnp.tanh(field_f)
        cohesion = 0.5 * jnp.exp(0.7 * jnp.tanh(0.5 * field_c))
        strength[i] = cohesion * horner(COSINE, t)
        sine[i] = horner(SINE, t)
        return 0

    lax.fori_loop(0, slabs, material, 0)

    half_step = 0.5 * time_step

    def move(i, _):
        for p in range(PIECES):
            top = TOP + p * rows
            at, up, down = pl.ds(top, rows), pl.ds(top - 1, rows), pl.ds(top + 1, rows)
            pull_u = suu[i + 1, at, :] - suu[i - 1, at, :] + (suw[i, down, :] - suw[i, up, :])
            pull_w = suw[i + 1, at, :] - suw[i - 1, at, :] + (sww[i, down, :] - sww[i, up, :])
            vu[i, at, :] = damping * vu[i, at, :] + half_step * pull_u
            vw[i, at, :] = damping * vw[i, at, :] + (half_step * pull_w - time_step * gravity)
        return 0

    def strain(i, _):
        for p in range(PIECES):
            top = TOP + p * rows
            at, up, down = pl.ds(top, rows), pl.ds(top - 1, rows), pl.ds(top + 1, rows)
            strain_uu = vu[i + 1, at, :] - vu[i - 1, at, :]
            strain_ww = vw[i, down, :] - vw[i, up, :]
            shear = vu[i, down, :] - vu[i, up, :] + (vw[i + 1, at, :] - vw[i - 1, at, :])
            s_uu, s_ww = suu[i, at, :], sww[i, at, :]
            middle = 0.5 * (s_uu + s_ww) + (0.5 * half_step * (modulus_m + modulus_l)) * (strain_uu + strain_ww)
            deviator = 0.5 * (s_uu - s_ww) + (0.5 * half_step * (modulus_m - modulus_l)) * (strain_uu - strain_ww)
            trial_uw = suw[i, at, :] + (half_step * modulus_g) * shear
            k = strength[i - 1, pl.ds(p * rows, rows), :]
            limit = jnp.maximum(k - middle * sine[i - 1, pl.ds(p * rows, rows), :], 0.1 * k)
            factor = jnp.minimum(limit * lax.rsqrt(deviator * deviator + trial_uw * trial_uw), 1.0)
            deviator = factor * deviator
            suu[i, at, :] = middle + deviator
            sww[i, at, :] = middle - deviator
            suw[i, at, :] = factor * trial_uw
        return 0

    def step(number, _):
        receive_x(0, (suu, suw))
        receive_y(0, (suw, sww))
        lax.fori_loop(1, slabs + 1, move, 0)
        send_x(1, (vu, vw))
        send_y(1, (vu, vw))
        receive_x(1, (vu, vw))
        receive_y(1, (vu, vw))
        lax.fori_loop(1, slabs + 1, strain, 0)

        @pl.when(number < STEPS - 1)
        def _():
            send_x(0, (suu, suw))
            send_y(0, (suw, sww))
        return 0

    lax.fori_loop(0, STEPS, step, 0)

    for field, result in ((vu, vu_out), (vw, vw_out), (suu, suu_out), (sww, sww_out), (suw, suw_out)):
        def back(i, _, field=field, result=result):
            result[pl.ds(i, LANES, stride=PART), :] = field[1 + i, whole, :].T
            return 0
        lax.fori_loop(0, slabs, back, 0)


def shards(mesh, velocity_u, velocity_w, stress_uu, stress_ww, stress_uw, basis, coefficients):
    realiz, cells_x, cells_y = velocity_u.shape
    n_chain, n_cross, n_real = mesh.shape["chain"], mesh.shape["cross"], mesh.shape["real"]
    modes = basis.shape[0] * n_real
    slabs = cells_x // PART
    sizes = (n_chain, n_cross, n_real, cells_x, cells_y, realiz, modes)
    flat = lambda x: x.reshape(-1, cells_y)
    tall = cells_y + 2 * TOP
    f32 = jnp.float32
    vmem = pl.BlockSpec(memory_space=pltpu.VMEM)
    dma = pltpu.SemaphoreType.DMA
    results = pl.pallas_call(
        functools.partial(kernel, sizes),
        out_shape=[jax.ShapeDtypeStruct((realiz * cells_x, cells_y), f32)] * 5,
        in_specs=[vmem] * 7,
        out_specs=[vmem] * 5,
        scratch_shapes=[pltpu.VMEM((slabs + 2, tall, LANES), f32)] * 5 + [
            pltpu.VMEM((slabs, cells_y, LANES), f32),
            pltpu.VMEM((slabs, cells_y, LANES), f32),
            pltpu.VMEM((modes * cells_x, cells_y), f32),
            pltpu.VMEM((2 * LANES, cells_y), f32),
            pltpu.VMEM((2, 2, cells_y // PIECES, LANES), f32),
            pltpu.VMEM((2, 2, cells_y // PIECES, LANES), f32),
            pltpu.VMEM((2, 2, 2 * slabs, LANES), f32),
            pltpu.VMEM((2, 2, 2 * slabs, LANES), f32),
            dma((2, 2)), dma((2, 2)), dma((2, 2)), dma((2, 2)),
            dma((n_real - 1,)), dma((n_real - 1,)), dma,
        ],
        compiler_params=pltpu.CompilerParams(
            collective_id=0, has_side_effects=True, vmem_limit_bytes=40 * 2**20),
    )(*[flat(x) for x in (velocity_u, velocity_w, stress_uu, stress_ww, stress_uw, basis)], coefficients)
    return tuple(x.reshape(realiz, cells_x, cells_y) for x in results)


def solution(mesh):
    block = P("real", "chain", "cross")
    return jax.shard_map(
        functools.partial(shards, mesh),
        mesh=mesh,
        in_specs=(block,) * 6 + (P(),),
        out_specs=(block,) * 5,
        check_vma=False,
    )
```

profile of v0, /device:TPU:0, one launch (start us, length us, event | category | flops | bytes accessed | tf_op | source)
XLA Modules:
  0.0 71.0 jit_solution(10806540494853542078)
XLA Ops:
  0.6 0.0 copy-start
  0.6 1.1 %copy-done = f32[24,64,128]{2,1,0:T(8,128)S(1)} copy-done((f32[24,64,128]{2,1,0:T(8,128)S(1)}, f32[24,64,128]{2,1,0:T(8,128)}, u32[]{:S(2)}) %copy-start) | copy-done | bytes 786456
  1.8 0.0 copy-start.1
  1.8 1.0 %copy-done.1 = f32[16,64,128]{2,1,0:T(8,128)S(1)} copy-done((f32[16,64,128]{2,1,0:T(8,128)S(1)}, f32[16,64,128]{2,1,0:T(8,128)}, u32[]{:S(2)}) %copy-start.1) | copy-done | bytes 524312
  2.8 0.0 copy-start.2
  2.8 1.0 %copy-done.2 = f32[16,64,128]{2,1,0:T(8,128)S(1)} copy-done((f32[16,64,128]{2,1,0:T(8,128)S(1)}, f32[16,64,128]{2,1,0:T(8,128)}, u32[]{:S(2)}) %copy-start.2) | copy-done | bytes 524312
  3.9 0.0 copy-start.3
  3.9 1.0 %copy-done.3 = f32[16,64,128]{2,1,0:T(8,128)S(1)} copy-done((f32[16,64,128]{2,1,0:T(8,128)S(1)}, f32[16,64,128]{2,1,0:T(8,128)}, u32[]{:S(2)}) %copy-start.3) | copy-done | bytes 524312
  4.9 0.0 copy-start.4
  4.9 1.0 %copy-done.4 = f32[16,64,128]{2,1,0:T(8,128)S(1)} copy-done((f32[16,64,128]{2,1,0:T(8,128)S(1)}, f32[16,64,128]{2,1,0:T(8,128)}, u32[]{:S(2)}) %copy-start.4) | copy-done | bytes 524312
  5.9 0.0 copy-start.5
  5.9 1.0 %copy-done.5 = f32[16,64,128]{2,1,0:T(8,128)S(1)} copy-done((f32[16,64,128]{2,1,0:T(8,128)S(1)}, f32[16,64,128]{2,1,0:T(8,128)}, u32[]{:S(2)}) %copy-start.5) | copy-done | bytes 524312
  7.0 0.0 copy-start.6
  7.0 0.8 %copy-done.6 = f32[2,32,48]{2,1,0:T(8,128)S(1)} copy-done((f32[2,32,48]{2,1,0:T(8,128)S(1)}, f32[2,32,48]{2,1,0:T(8,128)}, u32[]{:S(2)}) %copy-start.6) | copy-done | bytes 12312
  7.7 59.3 %shard_map.110 = (f32[1024,128]{1,0:T(8,128)S(1)}, f32[1024,128]{1,0:T(8,128)S(1)}, f32[1024,128]{1,0:T(8,128)S(1)}, f32[1024,128]{1,0:T(8,128)S(1)}, f32[1024,128]{1,0:T(8,128)S(1)}) custom-call(f32[1024,128]{1,0:T(8,128)S(1)} %bitcast.17, f32[1024,128]{1,0:T(8,128)S(1)} %bitcast.18, f32[1024,128]{1,0:T(8,128)S(1)} %bitcast.19, f32[1024,128]{1,0:T(8,128)S(1)} %bitcast.20, ...), custom_call_target="tpu_custom_call" | custom-call | tf_op jit(solution)/shard_map/pallas_call | solution.py:263
  67.1 0.8 %copy.17 = f32[16,64,128]{2,1,0:T(8,128)} copy(f32[16,64,128]{2,1,0:T(8,128)S(1)} %bitcast.16) | data formatting | bytes 1048576
  67.9 0.8 %copy.18 = f32[16,64,128]{2,1,0:T(8,128)} copy(f32[16,64,128]{2,1,0:T(8,128)S(1)} %bitcast.15) | data formatting | bytes 1048576
  68.7 0.8 %copy.19 = f32[16,64,128]{2,1,0:T(8,128)} copy(f32[16,64,128]{2,1,0:T(8,128)S(1)} %bitcast.14) | data formatting | bytes 1048576
  69.5 0.8 %copy.20 = f32[16,64,128]{2,1,0:T(8,128)} copy(f32[16,64,128]{2,1,0:T(8,128)S(1)} %bitcast.13) | data formatting | bytes 1048576
  70.2 0.8 %copy.21 = f32[16,64,128]{2,1,0:T(8,128)} copy(f32[16,64,128]{2,1,0:T(8,128)S(1)} %bitcast.12) | data formatting | bytes 1048576
Async XLA Ops:
  0.6 1.1 %copy-start = (f32[24,64,128]{2,1,0:T(8,128)S(1)}, f32[24,64,128]{2,1,0:T(8,128)}, u32[]{:S(2)}) copy-start(f32[24,64,128]{2,1,0:T(8,128)} %param.12) | copy-start | bytes 2359300
  1.8 1.0 %copy-start.1 = (f32[16,64,128]{2,1,0:T(8,128)S(1)}, f32[16,64,128]{2,1,0:T(8,128)}, u32[]{:S(2)}) copy-start(f32[16,64,128]{2,1,0:T(8,128)} %param.7) | copy-start | bytes 1572868
  2.8 1.0 %copy-start.2 = (f32[16,64,128]{2,1,0:T(8,128)S(1)}, f32[16,64,128]{2,1,0:T(8,128)}, u32[]{:S(2)}) copy-start(f32[16,64,128]{2,1,0:T(8,128)} %param.8) | copy-start | bytes 1572868
  3.9 1.0 %copy-start.3 = (f32[16,64,128]{2,1,0:T(8,128)S(1)}, f32[16,64,128]{2,1,0:T(8,128)}, u32[]{:S(2)}) copy-start(f32[16,64,128]{2,1,0:T(8,128)} %param.9) | copy-start | bytes 1572868
  4.9 1.0 %copy-start.4 = (f32[16,64,128]{2,1,0:T(8,128)S(1)}, f32[16,64,128]{2,1,0:T(8,128)}, u32[]{:S(2)}) copy-start(f32[16,64,128]{2,1,0:T(8,128)} %param.10) | copy-start | bytes 1572868
  5.9 1.0 %copy-start.5 = (f32[16,64,128]{2,1,0:T(8,128)S(1)}, f32[16,64,128]{2,1,0:T(8,128)}, u32[]{:S(2)}) copy-start(f32[16,64,128]{2,1,0:T(8,128)} %param.11) | copy-start | bytes 1572868
  7.0 0.8 %copy-start.6 = (f32[2,32,48]{2,1,0:T(8,128)S(1)}, f32[2,32,48]{2,1,0:T(8,128)}, u32[]{:S(2)}) copy-start(f32[2,32,48]{2,1,0:T(8,128)} %coef_in.1) | copy-start | bytes 36868
where the time goes:
time: 71.5 us; the launch traced here: 71 us
  Pallas kernels  59.3 us (83%)
  local copies, waits for them, and re-layouts  11.1 us (16%)
    pallas_call x1, Pallas kernels, shards(): pl.pallas_call(functools.partial(kernel, sizes), out_shape=[jax.ShapeDtyp...  59.3 us
    unnamed x19, local copies, waits for them, and re-layouts  11.1 us

commit v1 on v0

v1 whole, which is shorter than its diff:
```python
import functools
import math

import jax
import jax.numpy as jnp
from jax import lax
from jax.experimental import pallas as pl
from jax.experimental.pallas import tpu as pltpu
from jax.sharding import PartitionSpec as P

STEPS = 6
time_step = 0.8
damping = 0.8
gravity = 0.1
modulus_m = 1.8
modulus_l = 0.6
modulus_g = 0.6

MESH = pl.DeviceIdType.MESH
LANES = 128
PART = 8
TOP = 8
PIECES = 4

SINE = [(math.sin(0.6), math.cos(0.6), -math.sin(0.6), -math.cos(0.6))[n % 4] * 0.25**n / math.factorial(n) for n in range(8)]
COSINE = [(math.cos(0.6), -math.sin(0.6), -math.cos(0.6), math.sin(0.6))[n % 4] * 0.25**n / math.factorial(n) for n in range(8)]


def horner(coefs, t):
    total = jnp.full_like(t, coefs[-1])
    for c in coefs[-2::-1]:
        total = total * t + c
    return total


def kernel(
    sizes, vu_in, vw_in, suu_in, sww_in, suw_in, basis_in, coef_in,
    vu_out, vw_out, suu_out, sww_out, suw_out,
    vu, vw, suu, sww, suw, strength, sine, basis, panel, raw, coef,
    xsend, xrecv, ysend, yrecv, csend, crecv, turned, lines,
    xs_sem, xr_sem, ys_sem, yr_sem, cs_sem, cr_sem, bs_sem, br_sem, in_sem,
):
    n_chain, n_cross, n_real, cells_x, cells_y, realiz, modes = sizes
    slabs = cells_x // PART
    last = slabs
    rows = cells_y // PIECES
    ci, xi, ri = lax.axis_index("chain"), lax.axis_index("cross"), lax.axis_index("real")
    chain_has = (ci > 0, ci < n_chain - 1)
    cross_has = (xi > 0, xi < n_cross - 1)
    chain_to = (ci - 1, ci + 1)
    cross_to = (xi - 1, xi + 1)
    partners = [(chain_has[a], {"chain": chain_to[a]}) for a in range(2)]
    partners += [(cross_has[b], {"cross": cross_to[b]}) for b in range(2)]
    partners += [
        (jnp.logical_and(chain_has[a], cross_has[b]), {"chain": chain_to[a], "cross": cross_to[b]})
        for a in range(2) for b in range(2)]

    inputs = (suu_in, sww_in, suw_in, vu_in, vw_in)
    loads = [pltpu.make_async_copy(inputs[n], raw.at[n], in_sem.at[n]) for n in range(5)]
    for copy in loads:
        copy.start()
    coef_load = pltpu.make_async_copy(coef_in, coef, in_sem.at[5])
    coef_load.start()
    block = basis_in.shape[0]
    place = pl.ds(pl.multiple_of(ri * block, 8), block)
    own = pltpu.make_async_copy(basis_in, basis.at[place], in_sem.at[6])
    own.start()

    for buffer in (xrecv, yrecv, crecv, csend):
        buffer[...] = jnp.zeros_like(buffer)
    for field in (suw, sww):
        field[:, pl.ds(0, TOP), :] = jnp.zeros((slabs + 2, TOP, LANES), jnp.float32)
        field[:, pl.ds(TOP + cells_y, TOP), :] = jnp.zeros((slabs + 2, TOP, LANES), jnp.float32)

    barrier = pltpu.get_barrier_semaphore()
    greeted = n_real - 1
    for there, device in partners:
        @pl.when(there)
        def _(device=device):
            pl.semaphore_signal(barrier, inc=1, device_id=device, device_id_type=MESH)
        greeted = greeted + there.astype(jnp.int32)
    for d in range(1, n_real):
        pl.semaphore_signal(barrier, inc=1, device_id={"real": lax.rem(ri + d, n_real)}, device_id_type=MESH)
    pl.semaphore_wait(barrier, greeted)

    sends = []
    for d in range(1, n_real):
        copy = pltpu.make_async_remote_copy(
            basis_in, basis.at[place], bs_sem.at[d - 1], br_sem.at[d - 1],
            device_id={"real": lax.rem(ri + d, n_real)}, device_id_type=MESH)
        copy.start()
        sends.append(copy)

    slot_of = lax.broadcasted_iota(jnp.int32, (rows, LANES), 1) % PART
    slot_of_row = lax.broadcasted_iota(jnp.int32, (1, LANES), 1) % PART
    slot_of_line = lax.broadcasted_iota(jnp.int32, (slabs, LANES), 1) % PART
    line_of = lax.broadcasted_iota(jnp.int32, (slabs, LANES), 0)
    edges = (0, PART - 1)
    half_step = 0.5 * time_step
    signed = (half_step, -half_step)

    def copies(slot):
        found = []
        for n, (there, device) in enumerate(partners):
            if n < 2:
                source, target, out_sem, back_sem, mine, other = xsend, xrecv, xs_sem, xr_sem, (n,), (1 - n,)
            elif n < 4:
                source, target, out_sem, back_sem, mine, other = ysend, yrecv, ys_sem, yr_sem, (n - 2,), (3 - n,)
            else:
                p, q = (n - 4) // 2, (n - 4) % 2
                source, target, out_sem, back_sem, mine, other = csend, crecv, cs_sem, cr_sem, (p, q), (1 - p, 1 - q)
            make = lambda a, b: pltpu.make_async_remote_copy(
                source.at[(*a, slot)], target.at[(*b, slot)], out_sem.at[(*a, slot)], back_sem.at[(*b, slot)],
                device_id=device, device_id_type=MESH)
            found.append((there, make(mine, other), make(other, mine)))
        return found

    whole = pl.ds(TOP, cells_y)

    def piece(p):
        return pl.ds(TOP + p * rows, rows)

    def move(i, _):
        for p in range(PIECES):
            top = TOP + p * rows
            at, up, down = pl.ds(top, rows), pl.ds(top - 1, rows), pl.ds(top + 1, rows)
            pull_u = suu[i + 1, at, :] - suu[i - 1, at, :] + (suw[i, down, :] - suw[i, up, :])
            pull_w = suw[i + 1, at, :] - suw[i - 1, at, :] + (sww[i, down, :] - sww[i, up, :])
            vu[i, at, :] = damping * vu[i, at, :] + half_step * pull_u
            vw[i, at, :] = damping * vw[i, at, :] + (half_step * pull_w - time_step * gravity)
        return 0

    def strain(i, _):
        for p in range(PIECES):
            top = TOP + p * rows
            at, up, down = pl.ds(top, rows), pl.ds(top - 1, rows), pl.ds(top + 1, rows)
            strain_uu = vu[i + 1, at, :] - vu[i - 1, at, :]
            strain_ww = vw[i, down, :] - vw[i, up, :]
            shear = vu[i, down, :] - vu[i, up, :] + (vw[i + 1, at, :] - vw[i - 1, at, :])
            s_uu, s_ww = suu[i, at, :], sww[i, at, :]
            middle = 0.5 * (s_uu + s_ww) + (0.5 * half_step * (modulus_m + modulus_l)) * (strain_uu + strain_ww)
            deviator = 0.5 * (s_uu - s_ww) + (0.5 * half_step * (modulus_m - modulus_l)) * (strain_uu - strain_ww)
            trial_uw = suw[i, at, :] + (half_step * modulus_g) * shear
            k = strength[i - 1, pl.ds(p * rows, rows), :]
            limit = jnp.maximum(k - middle * sine[i - 1, pl.ds(p * rows, rows), :], 0.1 * k)
            factor = jnp.minimum(limit * lax.rsqrt(deviator * deviator + trial_uw * trial_uw), 1.0)
            deviator = factor * deviator
            suu[i, at, :] = middle + deviator
            sww[i, at, :] = middle - deviator
            suw[i, at, :] = factor * trial_uw
        return 0

    def prepare(slot):
        for t in range(2):
            for p in range(PIECES):
                for field in (suu, suw):
                    near = pltpu.roll(field[(last, 1)[t], piece(p), :], (1, LANES - 1)[t], 1)
                    field[(0, last + 1)[t], piece(p), :] = jnp.where(slot_of == edges[t], 0.0, near)
        lax.fori_loop(1, slabs + 1, move, 0)
        for t in range(2):
            slab = (1, last)[t]
            for group, fields in enumerate(((suu, suw), (vu, vw))):
                packed = jnp.zeros((rows, LANES), jnp.float32)
                for j in range(2 * PIECES):
                    part = fields[j // PIECES][slab, piece(j % PIECES), :]
                    shift = (j - edges[t]) % LANES
                    packed = jnp.where(slot_of == j, pltpu.roll(part, shift, 1) if shift else part, packed)
                xsend[t, slot, group] = packed
            row = (TOP, TOP + cells_y - 1)[t]
            for f, field in enumerate((suw, sww, vu, vw)):
                for i in range(slabs):
                    ysend[t, slot, pl.ds(f * slabs + i, 1), :] = field[1 + i, pl.ds(row, 1), :]
            for b in range(2):
                for k, field in enumerate((suu, suw, sww)):
                    csend[t, b, slot, pl.ds(k, 1), :] = field[slab, pl.ds((TOP, TOP + cells_y - 1)[b], 1), :]
        for there, copy, _ in copies(slot):
            @pl.when(there)
            def _(copy=copy):
                copy.start()

    def finish(slot):
        for there, copy, coming in copies(slot):
            @pl.when(there)
            def _(copy=copy, coming=coming):
                copy.wait_send()
                coming.wait_recv()
        for a in range(2):
            for b in range(2):
                turned[a, b] = pltpu.roll(crecv[a, b, slot], (LANES - PART + 1, PART - 1)[a], 1)
        for t in range(2):
            def got(f):
                return yrecv[t, slot, pl.ds(f * slabs, slabs), :]

            def mine(f):
                return ysend[t, slot, pl.ds(f * slabs, slabs), :]

            sg = signed[t]
            lines[pl.ds(0, slabs), :] = mine(2) - sg * got(0)
            lines[pl.ds(slabs, slabs), :] = mine(3) - sg * got(1)
            ghost_u = got(2) + sg * mine(0)
            ghost_w = got(3) + sg * mine(1)
            for a in range(2):
                here = jnp.logical_and(slot_of_line == edges[a], line_of == (0, slabs - 1)[a])
                ghost_u = ghost_u - jnp.where(here, signed[a] * turned[a, t, pl.ds(0, 1), :], 0.0)
                ghost_w = ghost_w - jnp.where(here, signed[a] * turned[a, t, pl.ds(1, 1), :], 0.0)
            there = cross_has[t].astype(jnp.float32)
            lines[pl.ds(2 * slabs, slabs), :] = ghost_u * there
            lines[pl.ds(3 * slabs, slabs), :] = ghost_w * there
            row, ghost = ((TOP, TOP - 1), (TOP + cells_y - 1, TOP + cells_y))[t]
            for f, (field, to) in enumerate(((vu, row), (vw, row), (vu, ghost), (vw, ghost))):
                for i in range(slabs):
                    field[1 + i, pl.ds(to, 1), :] = lines[pl.ds(f * slabs + i, 1), :]
        for t in range(2):
            slab, ghost, far = ((1, 0, last), (last, last + 1, 1))[t]
            sg = signed[t]
            there = chain_has[t].astype(jnp.float32)
            here = slot_of == edges[t]
            for p in range(PIECES):
                def theirs(group, f):
                    j = f * PIECES + p
                    shift = (edges[t] - j) % LANES
                    values = xrecv[t, slot, group]
                    return pltpu.roll(values, shift, 1) if shift else values

                at = piece(p)
                for f, (velocity, stress) in enumerate(((vu, suu), (vw, suw))):
                    now = velocity[slab, at, :]
                    velocity[slab, at, :] = jnp.where(here, now - sg * theirs(0, f), now)
                    outside = (theirs(1, f) + sg * stress[slab, at, :]) * there
                    near = pltpu.roll(velocity[far, at, :], (1, LANES - 1)[t], 1)
                    velocity[ghost, at, :] = jnp.where(here, outside, near)
            for b in range(2):
                row = pl.ds((TOP, TOP + cells_y - 1)[b], 1)
                for k, velocity in ((1, vu), (2, vw)):
                    fix = jnp.where(slot_of_row == edges[t], signed[b] * turned[t, b, pl.ds(k, 1), :], 0.0)
                    velocity[ghost, row, :] = velocity[ghost, row, :] - fix
        lax.fori_loop(1, slabs + 1, strain, 0)

    for n, field in enumerate((suu, sww, suw, vu, vw)):
        loads[n].wait()

        def turn(i, _, n=n, field=field):
            field[1 + i, whole, :] = raw[n, pl.ds(i, LANES, stride=PART), :].T
            return 0
        lax.fori_loop(0, slabs, turn, 0)
    prepare(0)

    coef_load.wait()
    own.wait()
    for copy in sends:
        copy.wait()
    weights = jnp.concatenate([coef[f, pl.ds(pl.multiple_of(ri * realiz, 8), realiz), :] for f in range(2)], axis=0)
    weights_high = weights.astype(jnp.bfloat16)
    weights_low = (weights - weights_high.astype(jnp.float32)).astype(jnp.bfloat16)
    both = jnp.concatenate([weights_high, weights_low], axis=0)
    half = 2 * realiz

    def material(i, _):
        for part in range(PART):
            values = basis[pl.ds(part * slabs + i, modes, stride=cells_x), :]
            high = values.astype(jnp.bfloat16)
            low = (values - high.astype(jnp.float32)).astype(jnp.bfloat16)
            product = jnp.dot(both, jnp.concatenate([high, low], axis=1), preferred_element_type=jnp.float32)
            sums = product[:half, :cells_y] + (product[:half, cells_y:] + product[half:, :cells_y])
            panel[pl.ds(part, half, stride=PART), :] = sums
        field_c = panel[pl.ds(0, LANES), :].T
        field_f = panel[pl.ds(LANES, LANES), :].T
        t = jnp.tanh(field_f)
        cohesion = 0.5 * jnp.exp(0.7 * jnp.tanh(0.5 * field_c))
        strength[i] = cohesion * horner(COSINE, t)
        sine[i] = horner(SINE, t)
        return 0

    lax.fori_loop(0, slabs, material, 0)

    def step(number, _):
        finish(number % 2)

        @pl.when(number < STEPS - 1)
        def _():
            prepare((number + 1) % 2)
        return 0

    lax.fori_loop(0, STEPS, step, 0)

    for field, result in ((vu, vu_out), (vw, vw_out), (suu, suu_out), (sww, sww_out), (suw, suw_out)):
        def back(i, _, field=field, result=result):
            result[pl.ds(i, LANES, stride=PART), :] = field[1 + i, whole, :].T
            return 0
        lax.fori_loop(0, slabs, back, 0)


def shards(mesh, velocity_u, velocity_w, stress_uu, stress_ww, stress_uw, basis, coefficients):
    realiz, cells_x, cells_y = velocity_u.shape
    n_chain, n_cross, n_real = mesh.shape["chain"], mesh.shape["cross"], mesh.shape["real"]
    modes = basis.shape[0] * n_real
    slabs = cells_x // PART
    sizes = (n_chain, n_cross, n_real, cells_x, cells_y, realiz, modes)
    flat = lambda x: x.reshape(-1, cells_y)
    tall = cells_y + 2 * TOP
    f32 = jnp.float32
    vmem = pl.BlockSpec(memory_space=pltpu.VMEM)
    dma = pltpu.SemaphoreType.DMA
    results = pl.pallas_call(
        functools.partial(kernel, sizes),
        out_shape=[jax.ShapeDtypeStruct((realiz * cells_x, cells_y), f32)] * 5,
        in_specs=[pl.BlockSpec(memory_space=pl.ANY)] * 7,
        out_specs=[vmem] * 5,
        scratch_shapes=[pltpu.VMEM((slabs + 2, tall, LANES), f32)] * 5 + [
            pltpu.VMEM((slabs, cells_y, LANES), f32),
            pltpu.VMEM((slabs, cells_y, LANES), f32),
            pltpu.VMEM((modes * cells_x, cells_y), f32),
            pltpu.VMEM((2 * LANES, cells_y), f32),
            pltpu.VMEM((5, realiz * cells_x, cells_y), f32),
            pltpu.VMEM(coefficients.shape, f32),
            pltpu.VMEM((2, 2, 2, cells_y // PIECES, LANES), f32),
            pltpu.VMEM((2, 2, 2, cells_y // PIECES, LANES), f32),
            pltpu.VMEM((2, 2, 4 * slabs, LANES), f32),
            pltpu.VMEM((2, 2, 4 * slabs, LANES), f32),
            pltpu.VMEM((2, 2, 2, 8, LANES), f32),
            pltpu.VMEM((2, 2, 2, 8, LANES), f32),
            pltpu.VMEM((2, 2, 8, LANES), f32),
            pltpu.VMEM((4 * slabs, LANES), f32),
            dma((2, 2)), dma((2, 2)), dma((2, 2)), dma((2, 2)), dma((2, 2, 2)), dma((2, 2, 2)),
            dma((n_real - 1,)), dma((n_real - 1,)), dma((7,)),
        ],
        compiler_params=pltpu.CompilerParams(
            collective_id=0, has_side_effects=True, vmem_limit_bytes=40 * 2**20),
    )(*[flat(x) for x in (velocity_u, velocity_w, stress_uu, stress_ww, stress_uw, basis)], coefficients)
    return tuple(x.reshape(realiz, cells_x, cells_y) for x in results)


def solution(mesh):
    block = P("real", "chain", "cross")
    return jax.shard_map(
        functools.partial(shards, mesh),
        mesh=mesh,
        in_specs=(block,) * 6 + (P(),),
        out_specs=(block,) * 5,
        check_vma=False,
    )
```

time: 71.5 us -> 59.6 us (0.83)
  Pallas kernels: 59.3 us -> 47.4 us
    pallas_call x1, Pallas kernels: 59.3 us -> 47.4 us  [shards(): pl.pallas_call(functools.partial(kernel, sizes), out_shape=[jax.ShapeDtyp...]
where the time goes in v1:
time: 59.6 us; the launch traced here: 59.1 us
  Pallas kernels  47.4 us (80%)
  local copies, waits for them, and re-layouts  11.1 us (19%)
  between operations  0.66 us (1%)
    pallas_call x1, Pallas kernels, shards(): pl.pallas_call(functools.partial(kernel, sizes), out_shape=[jax.ShapeDtyp...  47.4 us
    unnamed x19, local copies, waits for them, and re-layouts  11.1 us

profile of v1, /device:TPU:0, one launch (start us, length us, event | category | flops | bytes accessed | tf_op | source)
XLA Modules:
  0.0 59.1 jit_solution(13570810471668921361)
XLA Ops:
  0.6 0.0 copy-start
  0.6 1.1 %copy-done = f32[24,64,128]{2,1,0:T(8,128)S(1)} copy-done((f32[24,64,128]{2,1,0:T(8,128)S(1)}, f32[24,64,128]{2,1,0:T(8,128)}, u32[]{:S(2)}) %copy-start) | copy-done | bytes 786456
  1.8 0.0 copy-start.1
  1.8 1.0 %copy-done.1 = f32[16,64,128]{2,1,0:T(8,128)S(1)} copy-done((f32[16,64,128]{2,1,0:T(8,128)S(1)}, f32[16,64,128]{2,1,0:T(8,128)}, u32[]{:S(2)}) %copy-start.1) | copy-done | bytes 524312
  2.8 0.0 copy-start.2
  2.8 1.0 %copy-done.2 = f32[16,64,128]{2,1,0:T(8,128)S(1)} copy-done((f32[16,64,128]{2,1,0:T(8,128)S(1)}, f32[16,64,128]{2,1,0:T(8,128)}, u32[]{:S(2)}) %copy-start.2) | copy-done | bytes 524312
  3.9 0.0 copy-start.3
  3.9 1.0 %copy-done.3 = f32[16,64,128]{2,1,0:T(8,128)S(1)} copy-done((f32[16,64,128]{2,1,0:T(8,128)S(1)}, f32[16,64,128]{2,1,0:T(8,128)}, u32[]{:S(2)}) %copy-start.3) | copy-done | bytes 524312
  4.9 0.0 copy-start.4
  4.9 1.0 %copy-done.4 = f32[16,64,128]{2,1,0:T(8,128)S(1)} copy-done((f32[16,64,128]{2,1,0:T(8,128)S(1)}, f32[16,64,128]{2,1,0:T(8,128)}, u32[]{:S(2)}) %copy-start.4) | copy-done | bytes 524312
  5.9 0.0 copy-start.5
  5.9 1.0 %copy-done.5 = f32[16,64,128]{2,1,0:T(8,128)S(1)} copy-done((f32[16,64,128]{2,1,0:T(8,128)S(1)}, f32[16,64,128]{2,1,0:T(8,128)}, u32[]{:S(2)}) %copy-start.5) | copy-done | bytes 524312
  7.0 0.0 copy-start.6
  7.0 0.8 %copy-done.6 = f32[2,32,48]{2,1,0:T(8,128)S(1)} copy-done((f32[2,32,48]{2,1,0:T(8,128)S(1)}, f32[2,32,48]{2,1,0:T(8,128)}, u32[]{:S(2)}) %copy-start.6) | copy-done | bytes 12312
  7.7 47.4 %shard_map.110 = (f32[1024,128]{1,0:T(8,128)S(1)}, f32[1024,128]{1,0:T(8,128)S(1)}, f32[1024,128]{1,0:T(8,128)S(1)}, f32[1024,128]{1,0:T(8,128)S(1)}, f32[1024,128]{1,0:T(8,128)S(1)}) custom-call(f32[1024,128]{1,0:T(8,128)S(1)} %bitcast.17, f32[1024,128]{1,0:T(8,128)S(1)} %bitcast.18, f32[1024,128]{1,0:T(8,128)S(1)} %bitcast.19, f32[1024,128]{1,0:T(8,128)S(1)} %bitcast.20, ...), custom_call_target="tpu_custom_call" | custom-call | tf_op jit(solution)/shard_map/pallas_call | solution.py:304
  55.2 0.8 %copy.17 = f32[16,64,128]{2,1,0:T(8,128)} copy(f32[16,64,128]{2,1,0:T(8,128)S(1)} %bitcast.16) | data formatting | bytes 1048576
  56.0 0.8 %copy.18 = f32[16,64,128]{2,1,0:T(8,128)} copy(f32[16,64,128]{2,1,0:T(8,128)S(1)} %bitcast.15) | data formatting | bytes 1048576
  56.8 0.8 %copy.19 = f32[16,64,128]{2,1,0:T(8,128)} copy(f32[16,64,128]{2,1,0:T(8,128)S(1)} %bitcast.14) | data formatting | bytes 1048576
  57.5 0.8 %copy.20 = f32[16,64,128]{2,1,0:T(8,128)} copy(f32[16,64,128]{2,1,0:T(8,128)S(1)} %bitcast.13) | data formatting | bytes 1048576
  58.3 0.8 %copy.21 = f32[16,64,128]{2,1,0:T(8,128)} copy(f32[16,64,128]{2,1,0:T(8,128)S(1)} %bitcast.12) | data formatting | bytes 1048576
Async XLA Ops:
  0.6 1.1 %copy-start = (f32[24,64,128]{2,1,0:T(8,128)S(1)}, f32[24,64,128]{2,1,0:T(8,128)}, u32[]{:S(2)}) copy-start(f32[24,64,128]{2,1,0:T(8,128)} %param.12) | copy-start | bytes 2359300
  1.8 1.0 %copy-start.1 = (f32[16,64,128]{2,1,0:T(8,128)S(1)}, f32[16,64,128]{2,1,0:T(8,128)}, u32[]{:S(2)}) copy-start(f32[16,64,128]{2,1,0:T(8,128)} %param.7) | copy-start | bytes 1572868
  2.8 1.0 %copy-start.2 = (f32[16,64,128]{2,1,0:T(8,128)S(1)}, f32[16,64,128]{2,1,0:T(8,128)}, u32[]{:S(2)}) copy-start(f32[16,64,128]{2,1,0:T(8,128)} %param.8) | copy-start | bytes 1572868
  3.9 1.0 %copy-start.3 = (f32[16,64,128]{2,1,0:T(8,128)S(1)}, f32[16,64,128]{2,1,0:T(8,128)}, u32[]{:S(2)}) copy-start(f32[16,64,128]{2,1,0:T(8,128)} %param.9) | copy-start | bytes 1572868
  4.9 1.0 %copy-start.4 = (f32[16,64,128]{2,1,0:T(8,128)S(1)}, f32[16,64,128]{2,1,0:T(8,128)}, u32[]{:S(2)}) copy-start(f32[16,64,128]{2,1,0:T(8,128)} %param.10) | copy-start | bytes 1572868
  5.9 1.0 %copy-start.5 = (f32[16,64,128]{2,1,0:T(8,128)S(1)}, f32[16,64,128]{2,1,0:T(8,128)}, u32[]{:S(2)}) copy-start(f32[16,64,128]{2,1,0:T(8,128)} %param.11) | copy-start | bytes 1572868
  7.0 0.8 %copy-start.6 = (f32[2,32,48]{2,1,0:T(8,128)S(1)}, f32[2,32,48]{2,1,0:T(8,128)}, u32[]{:S(2)}) copy-start(f32[2,32,48]{2,1,0:T(8,128)} %coef_in.1) | copy-start | bytes 36868

commit v2 on v1

--- a/solution.py
+++ b/solution.py
@@ -35,7 +35,6 @@
 
 def kernel(
     sizes, vu_in, vw_in, suu_in, sww_in, suw_in, basis_in, coef_in,
-    vu_out, vw_out, suu_out, sww_out, suw_out,
     vu, vw, suu, sww, suw, strength, sine, basis, panel, raw, coef,
     xsend, xrecv, ysend, yrecv, csend, crecv, turned, lines,
     xs_sem, xr_sem, ys_sem, yr_sem, cs_sem, cr_sem, bs_sem, br_sem, in_sem,
@@ -151,12 +150,31 @@
         return 0
 
     def prepare(slot):
+        out = copies(slot)
+
+        def start(those):
+            for there, copy, _ in those:
+                @pl.when(there)
+                def _(copy=copy):
+                    copy.start()
+
+        for a in range(2):
+            for b in range(2):
+                for k, field in enumerate((suu, suw, sww)):
+                    csend[a, b, slot, pl.ds(k, 1), :] = field[(1, last)[a], pl.ds((TOP, TOP + cells_y - 1)[b], 1), :]
+        start(out[4:])
         for t in range(2):
             for p in range(PIECES):
                 for field in (suu, suw):
                     near = pltpu.roll(field[(last, 1)[t], piece(p), :], (1, LANES - 1)[t], 1)
                     field[(0, last + 1)[t], piece(p), :] = jnp.where(slot_of == edges[t], 0.0, near)
         lax.fori_loop(1, slabs + 1, move, 0)
+        for t in range(2):
+            row = (TOP, TOP + cells_y - 1)[t]
+            for f, field in enumerate((suw, sww, vu, vw)):
+                for i in range(slabs):
+                    ysend[t, slot, pl.ds(f * slabs + i, 1), :] = field[1 + i, pl.ds(row, 1), :]
+        start(out[2:4])
         for t in range(2):
             slab = (1, last)[t]
             for group, fields in enumerate(((suu, suw), (vu, vw))):
@@ -166,17 +184,7 @@
                     shift = (j - edges[t]) % LANES
                     packed = jnp.where(slot_of == j, pltpu.roll(part, shift, 1) if shift else part, packed)
                 xsend[t, slot, group] = packed
-            row = (TOP, TOP + cells_y - 1)[t]
-            for f, field in enumerate((suw, sww, vu, vw)):
-                for i in range(slabs):
-                    ysend[t, slot, pl.ds(f * slabs + i, 1), :] = field[1 + i, pl.ds(row, 1), :]
-            for b in range(2):
-                for k, field in enumerate((suu, suw, sww)):
-                    csend[t, b, slot, pl.ds(k, 1), :] = field[slab, pl.ds((TOP, TOP + cells_y - 1)[b], 1), :]
-        for there, copy, _ in copies(slot):
-            @pl.when(there)
-            def _(copy=copy):
-                copy.start()
+        start(out[:2])
 
     def finish(slot):
         for there, copy, coming in copies(slot):
@@ -238,11 +246,8 @@
 
     for n, field in enumerate((suu, sww, suw, vu, vw)):
         loads[n].wait()
-
-        def turn(i, _, n=n, field=field):
-            field[1 + i, whole, :] = raw[n, pl.ds(i, LANES, stride=PART), :].T
-            return 0
-        lax.fori_loop(0, slabs, turn, 0)
+        for i in range(slabs):
+            field[1 + i, whole, :] = raw[n, pl.ds(i, LANES, stride=slabs), :].T
     prepare(0)
 
     coef_load.wait()
@@ -283,11 +288,22 @@
 
     lax.fori_loop(0, STEPS, step, 0)
 
-    for field, result in ((vu, vu_out), (vw, vw_out), (suu, suu_out), (sww, sww_out), (suw, suw_out)):
-        def back(i, _, field=field, result=result):
-            result[pl.ds(i, LANES, stride=PART), :] = field[1 + i, whole, :].T
-            return 0
-        lax.fori_loop(0, slabs, back, 0)
+
+def turn_back(vu, vw, suu, sww, suw, vu_out, vw_out, suu_out, sww_out, suw_out, fields, held, load_sem, sem):
+    cells_y, slabs = held.shape[2], vu.shape[0] - 2
+    loads = [pltpu.make_async_copy(x, fields.at[n], load_sem.at[n]) for n, x in enumerate((vu, vw, suu, sww, suw))]
+    for copy in loads:
+        copy.start()
+    copies = []
+    for n, result in enumerate((vu_out, vw_out, suu_out, sww_out, suw_out)):
+        loads[n].wait()
+        for i in range(slabs):
+            held[n, pl.ds(i, LANES, stride=slabs), :] = fields[n, 1 + i, pl.ds(TOP, cells_y), :].T
+        copy = pltpu.make_async_copy(held.at[n], result, sem.at[n])
+        copy.start()
+        copies.append(copy)
+    for copy in copies:
+        copy.wait()
 
 
 def shards(mesh, velocity_u, velocity_w, stress_uu, stress_ww, stress_uw, basis, coefficients):
@@ -301,12 +317,12 @@
     f32 = jnp.float32
     vmem = pl.BlockSpec(memory_space=pltpu.VMEM)
     dma = pltpu.SemaphoreType.DMA
-    results = pl.pallas_call(
+    turned = pl.pallas_call(
         functools.partial(kernel, sizes),
-        out_shape=[jax.ShapeDtypeStruct((realiz * cells_x, cells_y), f32)] * 5,
-        in_specs=[pl.BlockSpec(memory_space=pl.ANY)] * 7,
+        out_shape=[jax.ShapeDtypeStruct((slabs + 2, tall, LANES), f32)] * 5,
+        in_specs=[pl.BlockSpec(memory_space=pltpu.HBM)] * 7,
         out_specs=[vmem] * 5,
-        scratch_shapes=[pltpu.VMEM((slabs + 2, tall, LANES), f32)] * 5 + [
+        scratch_shapes=[
             pltpu.VMEM((slabs, cells_y, LANES), f32),
             pltpu.VMEM((slabs, cells_y, LANES), f32),
             pltpu.VMEM((modes * cells_x, cells_y), f32),
@@ -325,8 +341,18 @@
             dma((n_real - 1,)), dma((n_real - 1,)), dma((7,)),
         ],
         compiler_params=pltpu.CompilerParams(
-            collective_id=0, has_side_effects=True, vmem_limit_bytes=40 * 2**20),
+            collective_id=0, has_side_effects=True, vmem_limit_bytes=62 * 2**20),
     )(*[flat(x) for x in (velocity_u, velocity_w, stress_uu, stress_ww, stress_uw, basis)], coefficients)
+    results = pl.pallas_call(
+        turn_back,
+        out_shape=[jax.ShapeDtypeStruct((realiz * cells_x, cells_y), f32)] * 5,
+        in_specs=[pl.BlockSpec(memory_space=pltpu.HBM)] * 5,
+        out_specs=[pl.BlockSpec(memory_space=pltpu.HBM)] * 5,
+        scratch_shapes=[
+            pltpu.VMEM((5, slabs + 2, tall, LANES), f32),
+            pltpu.VMEM((5, realiz * cells_x, cells_y), f32), dma((5,)), dma((5,))],
+        compiler_params=pltpu.CompilerParams(vmem_limit_bytes=62 * 2**20),
+    )(*turned)
     return tuple(x.reshape(realiz, cells_x, cells_y) for x in results)
 
 

time: 59.6 us -> 41.7 us (0.70)
  local copies, waits for them, and re-layouts: 11.1 us -> 0 us
  Pallas kernels: 47.4 us -> 40.9 us
    unnamed x19 -> x0, local copies, waits for them, and re-layouts: 11.1 us -> none
    pallas_call x1, Pallas kernels: 47.4 us -> 37.9 us  [shards(): pl.pallas_call(functools.partial(kernel, sizes), out_shape=[jax.ShapeDtyp...]
    pallas_call x0 -> x1, Pallas kernels: none -> 3.09 us  [shards(): pl.pallas_call(turn_back, out_shape=[jax.ShapeDtypeStruct((realiz * cells...]
where the time goes in v2:
time: 41.7 us; the launch traced here: 41.6 us
  Pallas kernels  40.9 us (98%)
  between operations  0.64 us (2%)
    pallas_call x1, Pallas kernels, shards(): pl.pallas_call(functools.partial(kernel, sizes), out_shape=[jax.ShapeDtyp...  37.9 us
    pallas_call x1, Pallas kernels, shards(): pl.pallas_call(turn_back, out_shape=[jax.ShapeDtypeStruct((realiz * cells...  3.09 us

profile of v2, /device:TPU:0, one launch (start us, length us, event | category | flops | bytes accessed | tf_op | source)
XLA Modules:
  0.0 41.6 jit_solution(8210108122575845460)
XLA Ops:
  0.6 37.9 %shard_map.110 = (f32[10,144,128]{2,1,0:T(8,128)}, f32[10,144,128]{2,1,0:T(8,128)}, f32[10,144,128]{2,1,0:T(8,128)}, f32[10,144,128]{2,1,0:T(8,128)}, f32[10,144,128]{2,1,0:T(8,128)}) custom-call(f32[1024,128]{1,0:T(8,128)} %bitcast.12, f32[1024,128]{1,0:T(8,128)} %bitcast.13, f32[1024,128]{1,0:T(8,128)} %bitcast.14, f32[1024,128]{1,0:T(8,128)} %bitcast.15, ...), custom_call_target="tpu_custom_call" | custom-call | tf_op jit(solution)/shard_map/pallas_call | solution.py:320
  38.5 3.1 %shard_map.111 = (f32[1024,128]{1,0:T(8,128)}, f32[1024,128]{1,0:T(8,128)}, f32[1024,128]{1,0:T(8,128)}, f32[1024,128]{1,0:T(8,128)}, f32[1024,128]{1,0:T(8,128)}) custom-call(f32[10,144,128]{2,1,0:T(8,128)} %get-tuple-element.15.vu, f32[10,144,128]{2,1,0:T(8,128)} %get-tuple-element.16.vw, f32[10,144,128]{2,1,0:T(8,128)} %get-tuple-element.17.suu, ...), custom_call_target="tpu_custom_call" | custom-call | tf_op jit(solution)/shard_map/pallas_call | solution.py:346

commit v3 on v2

--- a/solution.py
+++ b/solution.py
@@ -129,10 +129,10 @@
             vw[i, at, :] = damping * vw[i, at, :] + (half_step * pull_w - time_step * gravity)
         return 0
 
-    def strain(i, _):
-        for p in range(PIECES):
-            top = TOP + p * rows
-            at, up, down = pl.ds(top, rows), pl.ds(top - 1, rows), pl.ds(top + 1, rows)
+    def strain(i, pieces):
+        for first, count in pieces:
+            top = TOP + first
+            at, up, down = pl.ds(top, count), pl.ds(top - 1, count), pl.ds(top + 1, count)
             strain_uu = vu[i + 1, at, :] - vu[i - 1, at, :]
             strain_ww = vw[i, down, :] - vw[i, up, :]
             shear = vu[i, down, :] - vu[i, up, :] + (vw[i + 1, at, :] - vw[i - 1, at, :])
@@ -140,14 +140,19 @@
             middle = 0.5 * (s_uu + s_ww) + (0.5 * half_step * (modulus_m + modulus_l)) * (strain_uu + strain_ww)
             deviator = 0.5 * (s_uu - s_ww) + (0.5 * half_step * (modulus_m - modulus_l)) * (strain_uu - strain_ww)
             trial_uw = suw[i, at, :] + (half_step * modulus_g) * shear
-            k = strength[i - 1, pl.ds(p * rows, rows), :]
-            limit = jnp.maximum(k - middle * sine[i - 1, pl.ds(p * rows, rows), :], 0.1 * k)
+            k = strength[i - 1, pl.ds(first, count), :]
+            limit = jnp.maximum(k - middle * sine[i - 1, pl.ds(first, count), :], 0.1 * k)
             factor = jnp.minimum(limit * lax.rsqrt(deviator * deviator + trial_uw * trial_uw), 1.0)
             deviator = factor * deviator
             suu[i, at, :] = middle + deviator
             sww[i, at, :] = middle - deviator
             suw[i, at, :] = factor * trial_uw
         return 0
+
+    margin = 8
+    inner = [(y, min(rows, cells_y - margin - y)) for y in range(margin, cells_y - margin, rows)]
+    outer = [(0, margin), (cells_y - margin, margin)]
+    full = [(p * rows, rows) for p in range(PIECES)]
 
     def prepare(slot):
         out = copies(slot)
@@ -187,6 +192,7 @@
         start(out[:2])
 
     def finish(slot):
+        lax.fori_loop(3, slabs - 1, lambda i, _: strain(i, inner), 0)
         for there, copy, coming in copies(slot):
             @pl.when(there)
             def _(copy=copy, coming=coming):
@@ -242,7 +248,8 @@
                 for k, velocity in ((1, vu), (2, vw)):
                     fix = jnp.where(slot_of_row == edges[t], signed[b] * turned[t, b, pl.ds(k, 1), :], 0.0)
                     velocity[ghost, row, :] = velocity[ghost, row, :] - fix
-        lax.fori_loop(1, slabs + 1, strain, 0)
+        lax.fori_loop(3, slabs - 1, lambda i, _: strain(i, outer), 0)
+        lax.fori_loop(0, 4, lambda k, _: strain(1 + k + k // 2 * (slabs - 4), full), 0)
 
     for n, field in enumerate((suu, sww, suw, vu, vw)):
         loads[n].wait()

time: 41.7 us -> 40.5 us (0.971)
  Pallas kernels: 40.9 us -> 39.7 us
    pallas_call x1, Pallas kernels: 37.9 us -> 36.6 us  [shards(): pl.pallas_call(functools.partial(kernel, sizes), out_shape=[jax.ShapeDtyp...]
where the time goes in v3:
time: 40.5 us; the launch traced here: 40.3 us
  Pallas kernels  39.7 us (98%)
  between operations  0.64 us (2%)
    pallas_call x1, Pallas kernels, shards(): pl.pallas_call(functools.partial(kernel, sizes), out_shape=[jax.ShapeDtyp...  36.6 us
    pallas_call x1, Pallas kernels, shards(): pl.pallas_call(turn_back, out_shape=[jax.ShapeDtypeStruct((realiz * cells...  3.09 us

profile of v3, /device:TPU:0, one launch (start us, length us, event | category | flops | bytes accessed | tf_op | source)
XLA Modules:
  0.0 40.3 jit_solution(9416787220741166750)
XLA Ops:
  0.6 36.6 %shard_map.110 = (f32[10,144,128]{2,1,0:T(8,128)}, f32[10,144,128]{2,1,0:T(8,128)}, f32[10,144,128]{2,1,0:T(8,128)}, f32[10,144,128]{2,1,0:T(8,128)}, f32[10,144,128]{2,1,0:T(8,128)}) custom-call(f32[1024,128]{1,0:T(8,128)} %bitcast.12, f32[1024,128]{1,0:T(8,128)} %bitcast.13, f32[1024,128]{1,0:T(8,128)} %bitcast.14, f32[1024,128]{1,0:T(8,128)} %bitcast.15, ...), custom_call_target="tpu_custom_call" | custom-call | tf_op jit(solution)/shard_map/pallas_call | solution.py:327
  37.2 3.1 %shard_map.111 = (f32[1024,128]{1,0:T(8,128)}, f32[1024,128]{1,0:T(8,128)}, f32[1024,128]{1,0:T(8,128)}, f32[1024,128]{1,0:T(8,128)}, f32[1024,128]{1,0:T(8,128)}) custom-call(f32[10,144,128]{2,1,0:T(8,128)} %get-tuple-element.15.vu, f32[10,144,128]{2,1,0:T(8,128)} %get-tuple-element.16.vw, f32[10,144,128]{2,1,0:T(8,128)} %get-tuple-element.17.suu, ...), custom_call_target="tpu_custom_call" | custom-call | tf_op jit(solution)/shard_map/pallas_call | solution.py:353
